TPU v7x, 32 devices: a whole 2x2x4 slice. The times are simulated.
32 devices in a mesh: row: 8 (over y, x, core), col: 4 (over z).
Axes of the slice: x: 2, y: 2, z: 4, core: 2. Of those that a mesh axis runs over, the one named last changes fastest.
Arguments:
- video_rows: bfloat16 [12288, 1024], P(('row', 'col')), may hold values from -1.5 to 1.5
- video_ids: int32 [12288], P(('row', 'col')), may hold values from 0 to 767
- imu_rows: bfloat16 [12288, 1024], P(('row', 'col')), may hold values from -1.5 to 1.5
- imu_ids: int32 [12288], P(('row', 'col')), may hold values from 0 to 767
- audio_rows: bfloat16 [12288, 1024], P(('row', 'col')), may hold values from -1.5 to 1.5
- audio_ids: int32 [12288], P(('row', 'col')), may hold values from 0 to 767
- imu_log_scale: float32 [1], replicated, may hold values from 0 to 1
- imu_bias: float32 [1], replicated, may hold values from -3 to -1
- audio_log_scale: float32 [1], replicated, may hold values from 0 to 1
- audio_bias: float32 [1], replicated, may hold values from -3 to -1
Outputs:
- video_grad: float32 [12288, 1024], P(('row', 'col'))
- imu_grad: float32 [12288, 1024], P(('row', 'col'))
- audio_grad: float32 [12288, 1024], P(('row', 'col'))
- row_loss: float32 [12288], P(('row', 'col'))
All inputs are finite; a program needn't handle non-finite values.
Results may differ from a plain program's by a relative error of at most 0.0025.
Values may be sent and summed in bfloat16 or wider, within the bound.
No kernel may reach another device: no remote copies, remote signals or barrier semaphores. Data moves between devices by JAX's collectives and lax.ppermute only.
A program may use at most 128 MiB of HBM per device.

v0:
```python
import jax
import jax.numpy as jnp
from jax import lax
from jax.sharding import PartitionSpec as P

STEPS = 4


def passed_along(shard, axis, by):
    devices = lax.axis_size(axis)
    return lax.ppermute(shard, axis, [(i, (i + by) % devices) for i in range(devices)])


def weight_tile(video_block, video_tags, partner, partner_tags, scale, offset):
    products = lax.dot_general(
        video_block, partner, (((1,), (1,)), ((), ())), preferred_element_type=jnp.float32
    )
    logits = scale * products + offset
    signs = jnp.where(video_tags[:, None] == partner_tags[None, :], 1.0, -1.0).astype(logits.dtype)
    losses = jax.nn.softplus(-signs * logits)
    weighted = (-signs * jax.nn.sigmoid(-signs * logits) * scale).astype(jnp.bfloat16)
    return (losses, weighted)


def pair_tile(video_block, video_tags, partner, partner_tags, scale, offset):
    losses, weighted = weight_tile(video_block, video_tags, partner, partner_tags, scale, offset)
    video_term = jnp.dot(weighted, partner, preferred_element_type=jnp.float32)
    partner_term = lax.dot_general(
        weighted, video_block, (((0,), (0,)), ((), ())), preferred_element_type=jnp.float32
    )
    return (jnp.sum(losses, axis=1), video_term, partner_term)


def per_device(
    video_rows,
    video_ids,
    imu_rows,
    imu_ids,
    audio_rows,
    audio_ids,
    imu_log_scale,
    imu_bias,
    audio_log_scale,
    audio_bias,
):
    scale_imu = jnp.exp(imu_log_scale[0])
    scale_audio = jnp.exp(audio_log_scale[0])
    offset_imu = imu_bias[0]
    offset_audio = audio_bias[0]
    rows_here = video_rows.shape[0]
    width = video_rows.shape[1]
    imu_block, imu_tags = (imu_rows, imu_ids)
    audio_block, audio_tags = (audio_rows, audio_ids)
    loss_sum = jnp.zeros((rows_here,), jnp.float32)
    video_acc = jnp.zeros((rows_here, width), jnp.float32)
    imu_acc = jnp.zeros((rows_here, width), jnp.float32)
    audio_acc = jnp.zeros((rows_here, width), jnp.float32)
    for rotation in range(STEPS):
        if rotation > 0:
            imu_block, imu_tags = passed_along((imu_block, imu_tags), "row", 1)
            audio_block, audio_tags = passed_along((audio_block, audio_tags), "col", 1)
        loss_imu, video_imu, imu_term = pair_tile(
            video_rows, video_ids, imu_block, imu_tags, scale_imu, offset_imu
        )
        loss_audio, video_audio, audio_term = pair_tile(
            video_rows, video_ids, audio_block, audio_tags, scale_audio, offset_audio
        )
        loss_sum = loss_sum + (loss_imu + loss_audio)
        video_acc = video_acc + (video_imu + video_audio)
        imu_acc = imu_acc + imu_term
        audio_acc = audio_acc + audio_term
        if rotation < STEPS - 1:
            imu_acc = passed_along(imu_acc, "row", 1)
            audio_acc = passed_along(audio_acc, "col", 1)
        else:
            imu_acc = passed_along(imu_acc, "row", -(STEPS - 1))
            audio_acc = passed_along(audio_acc, "col", -(STEPS - 1))
    row_loss = loss_sum / (2.0 * STEPS * rows_here)
    return (video_acc, imu_acc, audio_acc, row_loss)


def solution(mesh):
    in_specs = (
        P(("row", "col"), None),
        P(("row", "col")),
        P(("row", "col"), None),
        P(("row", "col")),
        P(("row", "col"), None),
        P(("row", "col")),
        P(),
        P(),
        P(),
        P(),
    )
    out_specs = (
        P(("row", "col"), None),
        P(("row", "col"), None),
        P(("row", "col"), None),
        P(("row", "col")),
    )
    return jax.shard_map(
        per_device, mesh=mesh, in_specs=in_specs, out_specs=out_specs, check_vma=False
    )
```

profile of v0, /device:TPU:0, one launch (start us, length us, event | category | flops | bytes accessed | tf_op | source)
XLA Modules:
  0.0 216.4 jit_solution(3733387268900332076)
XLA Ops:
  0.6 0.0 copy-start
  0.6 3.1 %collective-permute-start.3 = (bf16[384,1024]{1,0:T(8,128)(2,1)}, bf16[384,1024]{1,0:T(8,128)(2,1)S(1)}, u32[]{:S(2)}, u32[]{:S(2)}) collective-permute-start(bf16[384,1024]{1,0:T(8,128)(2,1)} %param.14), channel_id=1, source_target_pairs={{0,1},{1,2},{2,3},{3,0},{4,5},{5,6},{6,7},{7,4},{8,9},{9,10},{10,1... | collective-permute-start | bytes 2359304 | tf_op jit(solution)/shard_map/ppermute | solution.py:11
  5.1 2.1 fusion.16
  7.2 0.0 copy-start.3
  7.2 0.0 copy-start.5
  7.2 0.7 fusion.24
  7.9 0.1 collective-permute-start.12
  9.3 0.9 fusion.17
  10.3 0.0 copy-start.2
  10.3 0.7 fusion.26
  11.0 1.6 collective-permute-start.16
  12.6 1.3 collective-permute-start.1
  13.9 1.6 collective-permute-start.2
  15.5 41.7 %collective-permute-done.2 = s32[384]{0:T(512)S(1)} collective-permute-done((s32[384]{0:T(512)S(1)}, s32[384]{0:T(512)S(1)}, u32[]{:S(2)}, u32[]{:S(2)}) %collective-permute-start.2) | collective-permute-done | bytes 1568 | tf_op jit(solution)/shard_map/ppermute | solution.py:11
  57.3 0.0 collective-permute-start
  57.3 0.0 collective-permute-done.3
  57.3 0.0 collective-permute-start.7
  57.3 0.9 fusion.19
  58.2 3.0 %collective-permute-done = s32[384]{0:T(512)S(1)} collective-permute-done((s32[384]{0:T(512)S(1)}, s32[384]{0:T(512)S(1)}, u32[]{:S(2)}, u32[]{:S(2)}) %collective-permute-start) | collective-permute-done | bytes 1568 | tf_op jit(solution)/shard_map/ppermute | solution.py:11
  61.2 0.0 collective-permute-done.1
  61.2 0.9 fusion.18
  62.1 0.0 collective-permute-done.12
  62.1 0.7 convolution_add_fusion.1
  62.8 0.1 collective-permute-start.13
  62.9 0.7 convolution_add_fusion
  63.6 0.1 collective-permute-start.17
  63.7 0.7 collective-permute-start.5
  64.4 0.9 collective-permute-start.6
  65.3 0.7 fusion.25
  66.1 46.6 %collective-permute-done.6 = s32[384]{0:T(512)S(1)} collective-permute-done((s32[384]{0:T(512)S(1)}, s32[384]{0:T(512)S(1)}, u32[]{:S(2)}, u32[]{:S(2)}) %collective-permute-start.6) | collective-permute-done | bytes 1568 | tf_op jit(solution)/shard_map/ppermute | solution.py:11
  112.6 0.4 collective-permute-start.4
  113.0 0.0 collective-permute-done.7
  113.0 0.0 collective-permute-start.11
  113.1 0.9 fusion.21
  114.0 2.6 %collective-permute-done.4 = s32[384]{0:T(512)S(1)} collective-permute-done((s32[384]{0:T(512)S(1)}, s32[384]{0:T(512)S(1)}, u32[]{:S(2)}, u32[]{:S(2)}) %collective-permute-start.4) | collective-permute-done | bytes 1568 | tf_op jit(solution)/shard_map/ppermute | solution.py:11
  116.6 0.0 collective-permute-done.5
  116.6 0.9 fusion.20
  117.5 0.7 fusion.32
  118.2 0.1 collective-permute-start.14
  118.3 0.7 fusion.35
  119.0 0.1 collective-permute-start.18
  119.1 0.8 fusion.27
  119.8 0.1 collective-permute-start.10
  119.9 0.9 collective-permute-start.9
  120.8 0.8 fusion.28
  121.5 0.7 fusion.29
  122.3 46.5 %collective-permute-done.10 = s32[384]{0:T(512)S(1)} collective-permute-done((s32[384]{0:T(512)S(1)}, s32[384]{0:T(512)S(1)}, u32[]{:S(2)}, u32[]{:S(2)}) %collective-permute-start.10) | collective-permute-done | bytes 1568 | tf_op jit(solution)/shard_map/ppermute | solution.py:11
  168.8 0.1 collective-permute-start.8
  168.9 0.9 fusion.23
  169.8 2.9 %collective-permute-done.8 = s32[384]{0:T(512)S(1)} collective-permute-done((s32[384]{0:T(512)S(1)}, s32[384]{0:T(512)S(1)}, u32[]{:S(2)}, u32[]{:S(2)}) %collective-permute-start.8) | collective-permute-done | bytes 1568 | tf_op jit(solution)/shard_map/ppermute | solution.py:11
  172.7 0.9 fusion.22
  173.6 0.7 fusion.37
  174.3 0.1 collective-permute-start.15
  174.4 0.7 fusion.40
  175.1 0.1 collective-permute-start.19
  175.2 0.7 fusion.31
  175.9 0.7 fusion.34
  176.7 0.6 add_multiply_fusion
  177.3 0.7 fusion.39
  178.0 2.2 %add_add_fusion = f32[384,1024]{1,0:T(8,128)} fusion(f32[384,1024]{1,0:T(8,128)S(1)} %fusion.39, f32[384,1024]{1,0:T(8,128)S(1)} %fusion.31, f32[384,1024]{1,0:T(8,128)S(1)} %fusion.34, f32[384,1024]{1,0:T(8,128)S(1)} %fusion.28, f32[384,1024]{1,0:T(8,128)S(1)} %fusion.29, f32[384,1024]{1,0:T(8,128)S(1)} %fusion.25, f32[384,1024]{1,0:T(8,128)S(1)} %fusion.27, ...), kind=kOutput, calls=%fused_computation.8 | convolution fusion | flops 306069504 | bytes 13962244 | tf_op jit(solution)/shard_map/dot_general | solution.py:27
  180.2 14.0 %collective-permute-done.15 = f32[384,1024]{1,0:T(8,128)S(1)} collective-permute-done((f32[384,1024]{1,0:T(8,128)S(1)}, f32[384,1024]{1,0:T(8,128)S(1)}, u32[]{:S(2)}, u32[]{:S(2)}) %collective-permute-start.15) | collective-permute-done | bytes 1572896 | tf_op jit(solution)/shard_map/ppermute | solution.py:11
  194.2 19.9 %collective-permute-done.19 = f32[384,1024]{1,0:T(8,128)S(1)} collective-permute-done((f32[384,1024]{1,0:T(8,128)S(1)}, f32[384,1024]{1,0:T(8,128)S(1)}, u32[]{:S(2)}, u32[]{:S(2)}) %collective-permute-start.19) | collective-permute-done | bytes 1572896 | tf_op jit(solution)/shard_map/ppermute | solution.py:11
  214.1 1.1 copy.20
  215.3 1.1 copy.21
  (15 shorter events, 0.0 us)
Async XLA Ops:
  0.6 4.4 %copy-start = (bf16[384,1024]{1,0:T(8,128)(2,1)S(1)}, bf16[384,1024]{1,0:T(8,128)(2,1)}, u32[]{:S(2)}) copy-start(bf16[384,1024]{1,0:T(8,128)(2,1)} %param.10) | copy-start | bytes 2359300
  0.6 56.6 %collective-permute-start.3 = (bf16[384,1024]{1,0:T(8,128)(2,1)}, bf16[384,1024]{1,0:T(8,128)(2,1)S(1)}, u32[]{:S(2)}, u32[]{:S(2)}) collective-permute-start(bf16[384,1024]{1,0:T(8,128)(2,1)} %param.14), channel_id=1, source_target_pairs={{0,1},{1,2},{2,3},{3,0},{4,5},{5,6},{6,7},{7,4},{8,9},{9,10},{10,1... | collective-permute-start | bytes 2359304 | tf_op jit(solution)/shard_map/ppermute | solution.py:11
  5.1 2.1 copy-start.1
  5.1 2.1 copy-start.4
  7.2 2.1 copy-start.3
  7.2 2.1 copy-start.5
  7.9 54.2 %collective-permute-start.12 = (f32[384,1024]{1,0:T(8,128)S(1)}, f32[384,1024]{1,0:T(8,128)S(1)}, u32[]{:S(2)}, u32[]{:S(2)}) collective-permute-start(f32[384,1024]{1,0:T(8,128)S(1)} %fusion.24), channel_id=1, source_target_pairs={{0,4},{4,8},{8,12},{12,16},{16,20},{20,24},{24,28},{28,0},{1,5},{5... | collective-permute-start | bytes 4718600 | tf_op jit(solution)/shard_map/ppermute | solution.py:11
  10.3 2.3 %copy-start.2 = (bf16[384,1024]{1,0:T(8,128)(2,1)S(1)}, bf16[384,1024]{1,0:T(8,128)(2,1)}, u32[]{:S(2)}) copy-start(bf16[384,1024]{1,0:T(8,128)(2,1)} %param.12) | copy-start | bytes 2359300
  11.0 51.9 %collective-permute-start.16 = (f32[384,1024]{1,0:T(8,128)S(1)}, f32[384,1024]{1,0:T(8,128)S(1)}, u32[]{:S(2)}, u32[]{:S(2)}) collective-permute-start(f32[384,1024]{1,0:T(8,128)S(1)} %fusion.26), channel_id=1, source_target_pairs={{0,1},{1,2},{2,3},{3,0},{4,5},{5,6},{6,7},{7,4},{8,9},{9,10},{10,1... | collective-permute-start | bytes 4718600 | tf_op jit(solution)/shard_map/ppermute | solution.py:11
  12.6 48.6 %collective-permute-start.1 = (bf16[384,1024]{1,0:T(8,128)(2,1)S(1)}, bf16[384,1024]{1,0:T(8,128)(2,1)S(1)}, u32[]{:S(2)}, u32[]{:S(2)}) collective-permute-start(bf16[384,1024]{1,0:T(8,128)(2,1)S(1)} %copy-done.2), channel_id=1, source_target_pairs={{0,4},{4,8},{8,12},{12,16},{16,20},{20,24},{24,28},{28,0},{1,5},{5... | collective-permute-start | bytes 2359304 | tf_op jit(solution)/shard_map/ppermute | solution.py:11
  13.9 43.3 %collective-permute-start.2 = (s32[384]{0:T(512)S(1)}, s32[384]{0:T(512)S(1)}, u32[]{:S(2)}, u32[]{:S(2)}) collective-permute-start(s32[384]{0:T(512)S(1)} %copy-done.5), channel_id=1, source_target_pairs={{0,1},{1,2},{2,3},{3,0},{4,5},{5,6},{6,7},{7,4},{8,9},{9,10},{10,1... | collective-permute-start | bytes 4616 | tf_op jit(solution)/shard_map/ppermute | solution.py:11
  57.3 3.9 %collective-permute-start = (s32[384]{0:T(512)S(1)}, s32[384]{0:T(512)S(1)}, u32[]{:S(2)}, u32[]{:S(2)}) collective-permute-start(s32[384]{0:T(512)S(1)} %copy-done.4), channel_id=1, source_target_pairs={{0,4},{4,8},{8,12},{12,16},{16,20},{20,24},{24,28},{28,0},{1,5},{5... | collective-permute-start | bytes 4616 | tf_op jit(solution)/shard_map/ppermute | solution.py:11
  57.3 55.8 %collective-permute-start.7 = (bf16[384,1024]{1,0:T(8,128)(2,1)S(1)}, bf16[384,1024]{1,0:T(8,128)(2,1)S(1)}, u32[]{:S(2)}, u32[]{:S(2)}) collective-permute-start(bf16[384,1024]{1,0:T(8,128)(2,1)S(1)} %collective-permute-done.3), channel_id=1, source_target_pairs={{0,1},{1,2},{2,3},{3,0},{4,5},{5,6},{6,7},{7,4},{8,9},{9,10},{10,1... | collective-permute-start | bytes 2359304 | tf_op jit(solution)/shard_map/ppermute | solution.py:11
  62.8 54.7 %collective-permute-start.13 = (f32[384,1024]{1,0:T(8,128)S(1)}, f32[384,1024]{1,0:T(8,128)S(1)}, u32[]{:S(2)}, u32[]{:S(2)}) collective-permute-start(f32[384,1024]{1,0:T(8,128)S(1)} %convolution_add_fusion.1), channel_id=1, source_target_pairs={{0,4},{4,8},{8,12},{12,16},{16,20},{20,24},{24,28},{28,0},{1,5},{5... | collective-permute-start | bytes 4718600 | tf_op jit(solution)/shard_map/ppermute | solution.py:11
  63.6 54.7 %collective-permute-start.17 = (f32[384,1024]{1,0:T(8,128)S(1)}, f32[384,1024]{1,0:T(8,128)S(1)}, u32[]{:S(2)}, u32[]{:S(2)}) collective-permute-start(f32[384,1024]{1,0:T(8,128)S(1)} %convolution_add_fusion), channel_id=1, source_target_pairs={{0,1},{1,2},{2,3},{3,0},{4,5},{5,6},{6,7},{7,4},{8,9},{9,10},{10,1... | collective-permute-start | bytes 4718600 | tf_op jit(solution)/shard_map/ppermute | solution.py:11
  63.7 52.9 %collective-permute-start.5 = (bf16[384,1024]{1,0:T(8,128)(2,1)S(1)}, bf16[384,1024]{1,0:T(8,128)(2,1)S(1)}, u32[]{:S(2)}, u32[]{:S(2)}) collective-permute-start(bf16[384,1024]{1,0:T(8,128)(2,1)S(1)} %collective-permute-done.1), channel_id=1, source_target_pairs={{0,4},{4,8},{8,12},{12,16},{16,20},{20,24},{24,28},{28,0},{1,5},{5... | collective-permute-start | bytes 2359304 | tf_op jit(solution)/shard_map/ppermute | solution.py:11
  64.4 48.2 %collective-permute-start.6 = (s32[384]{0:T(512)S(1)}, s32[384]{0:T(512)S(1)}, u32[]{:S(2)}, u32[]{:S(2)}) collective-permute-start(s32[384]{0:T(512)S(1)} %collective-permute-done.2), channel_id=1, source_target_pairs={{0,1},{1,2},{2,3},{3,0},{4,5},{5,6},{6,7},{7,4},{8,9},{9,10},{10,1... | collective-permute-start | bytes 4616 | tf_op jit(solution)/shard_map/ppermute | solution.py:11
  112.6 3.9 %collective-permute-start.4 = (s32[384]{0:T(512)S(1)}, s32[384]{0:T(512)S(1)}, u32[]{:S(2)}, u32[]{:S(2)}) collective-permute-start(s32[384]{0:T(512)S(1)} %collective-permute-done), channel_id=1, source_target_pairs={{0,4},{4,8},{8,12},{12,16},{16,20},{20,24},{24,28},{28,0},{1,5},{5... | collective-permute-start | bytes 4616 | tf_op jit(solution)/shard_map/ppermute | solution.py:11
  113.0 55.8 %collective-permute-start.11 = (bf16[384,1024]{1,0:T(8,128)(2,1)S(1)}, bf16[384,1024]{1,0:T(8,128)(2,1)S(1)}, u32[]{:S(2)}, u32[]{:S(2)}) collective-permute-start(bf16[384,1024]{1,0:T(8,128)(2,1)S(1)} %collective-permute-done.7), channel_id=1, source_target_pairs={{0,1},{1,2},{2,3},{3,0},{4,5},{5,6},{6,7},{7,4},{8,9},{9,10},{10,1... | collective-permute-start | bytes 2359304 | tf_op jit(solution)/shard_map/ppermute | solution.py:11
  118.2 55.4 %collective-permute-start.14 = (f32[384,1024]{1,0:T(8,128)S(1)}, f32[384,1024]{1,0:T(8,128)S(1)}, u32[]{:S(2)}, u32[]{:S(2)}) collective-permute-start(f32[384,1024]{1,0:T(8,128)S(1)} %fusion.32), channel_id=1, source_target_pairs={{0,4},{4,8},{8,12},{12,16},{16,20},{20,24},{24,28},{28,0},{1,5},{5... | collective-permute-start | bytes 4718600 | tf_op jit(solution)/shard_map/ppermute | solution.py:11
  119.0 55.4 %collective-permute-start.18 = (f32[384,1024]{1,0:T(8,128)S(1)}, f32[384,1024]{1,0:T(8,128)S(1)}, u32[]{:S(2)}, u32[]{:S(2)}) collective-permute-start(f32[384,1024]{1,0:T(8,128)S(1)} %fusion.35), channel_id=1, source_target_pairs={{0,1},{1,2},{2,3},{3,0},{4,5},{5,6},{6,7},{7,4},{8,9},{9,10},{10,1... | collective-permute-start | bytes 4718600 | tf_op jit(solution)/shard_map/ppermute | solution.py:11
  119.8 49.0 %collective-permute-start.10 = (s32[384]{0:T(512)S(1)}, s32[384]{0:T(512)S(1)}, u32[]{:S(2)}, u32[]{:S(2)}) collective-permute-start(s32[384]{0:T(512)S(1)} %collective-permute-done.6), channel_id=1, source_target_pairs={{0,1},{1,2},{2,3},{3,0},{4,5},{5,6},{6,7},{7,4},{8,9},{9,10},{10,1... | collective-permute-start | bytes 4616 | tf_op jit(solution)/shard_map/ppermute | solution.py:11
  119.9 52.8 %collective-permute-start.9 = (bf16[384,1024]{1,0:T(8,128)(2,1)S(1)}, bf16[384,1024]{1,0:T(8,128)(2,1)S(1)}, u32[]{:S(2)}, u32[]{:S(2)}) collective-permute-start(bf16[384,1024]{1,0:T(8,128)(2,1)S(1)} %collective-permute-done.5), channel_id=1, source_target_pairs={{0,4},{4,8},{8,12},{12,16},{16,20},{20,24},{24,28},{28,0},{1,5},{5... | collective-permute-start | bytes 2359304 | tf_op jit(solution)/shard_map/ppermute | solution.py:11
  168.8 3.9 %collective-permute-start.8 = (s32[384]{0:T(512)S(1)}, s32[384]{0:T(512)S(1)}, u32[]{:S(2)}, u32[]{:S(2)}) collective-permute-start(s32[384]{0:T(512)S(1)} %collective-permute-done.4), channel_id=1, source_target_pairs={{0,4},{4,8},{8,12},{12,16},{16,20},{20,24},{24,28},{28,0},{1,5},{5... | collective-permute-start | bytes 4616 | tf_op jit(solution)/shard_map/ppermute | solution.py:11
  174.3 19.9 %collective-permute-start.15 = (f32[384,1024]{1,0:T(8,128)S(1)}, f32[384,1024]{1,0:T(8,128)S(1)}, u32[]{:S(2)}, u32[]{:S(2)}) collective-permute-start(f32[384,1024]{1,0:T(8,128)S(1)} %fusion.37), channel_id=1, source_target_pairs={{0,20},{4,24},{8,28},{12,0},{16,4},{20,8},{24,12},{28,16},{1,21},{... | collective-permute-start | bytes 4718600 | tf_op jit(solution)/shard_map/ppermute | solution.py:11
  175.1 39.0 %collective-permute-start.19 = (f32[384,1024]{1,0:T(8,128)S(1)}, f32[384,1024]{1,0:T(8,128)S(1)}, u32[]{:S(2)}, u32[]{:S(2)}) collective-permute-start(f32[384,1024]{1,0:T(8,128)S(1)} %fusion.40), channel_id=1, source_target_pairs={{0,1},{1,2},{2,3},{3,0},{4,5},{5,6},{6,7},{7,4},{8,9},{9,10},{10,1... | collective-permute-start | bytes 4718600 | tf_op jit(solution)/shard_map/ppermute | solution.py:11
where the time goes:
time: 217 us; the launch traced here: 216 us
  waiting for transfers between devices  177 us (82%)
  matrix products  21.5 us (10%)
  starting transfers between devices  11.2 us (5%)
  between operations  3.64 us (2%)
  local copies, waits for them, and re-layouts  2.32 us (1%)
    ppermute x20, waiting for transfers between devices, passed_along(): lax.ppermute(shard, axis, [(i, (i + by) % devices) for i in range(devices)])  177 us
    ppermute x20, starting transfers between devices, passed_along(): lax.ppermute(shard, axis, [(i, (i + by) % devices) for i in range(devices)])  11.2 us
    dot_general x8, matrix products, weight_tile(): lax.dot_general(video_block, partner, (((1,), (1,)), ((), ())), preferred...  8.5 us
    dot_general x8, matrix products, pair_tile(): video_term = jnp.dot(weighted, partner, preferred_element_type=jnp.float32)  7.4 us
    dot_general x8, matrix products, pair_tile(): lax.dot_general(weighted, video_block, (((0,), (0,)), ((), ())), preferre...  5.6 us
  transfers between devices with their start and end apart: 20, of which 8 were waited for; matrix products, arithmetic and copies ran while one was open for 10% of the time, Pallas kernels for 0%

commit v1 on v0

v1 whole, which is shorter than its diff:
```python
import jax
import jax.numpy as jnp
from jax import lax
from jax.sharding import PartitionSpec as P

STEPS = 4
CHUNKS = 2


def passed_along(shard, axis, by):
    devices = lax.axis_size(axis)
    return lax.ppermute(shard, axis, [(i, (i + by) % devices) for i in range(devices)])


def along(shard, axis, pairs):
    return lax.ppermute(shard, axis, pairs)


def weights(video, video_tags, partner, partner_tags, scale, offset):
    products = lax.dot_general(
        video, partner, (((1,), (1,)), ((), ())), preferred_element_type=jnp.float32
    )
    logits = scale * products + offset
    signs = jnp.where(video_tags[:, None] == partner_tags[None, :], 1.0, -1.0)
    losses = jax.nn.softplus(-signs * logits)
    weighted = (-signs * jax.nn.sigmoid(-signs * logits) * scale).astype(jnp.bfloat16)
    return losses, weighted


def to_video(weighted, partner):
    return jnp.dot(weighted, partner, preferred_element_type=jnp.float32)


def to_partner(weighted, video):
    return lax.dot_general(
        weighted, video, (((0,), (0,)), ((), ())), preferred_element_type=jnp.float32
    )


def row_sum(losses):
    return jnp.sum(losses, axis=1)


def imu_exchange(video, video_tags, imu, imu_tags):
    devices = lax.axis_size("row")
    swap = [(r, r ^ 1) for r in range(devices)]

    def mixed(even, odd):
        return [(r, (r + (odd if r % 2 else even)) % devices) for r in range(devices)]

    imu_two = passed_along((imu, imu_tags), "row", 2)
    video_two = passed_along((video, video_tags), "row", -2)
    imu_mixed = along((imu, imu_tags), "row", mixed(1, 3))
    video_mixed = along((video, video_tags), "row", mixed(-3, -1))
    imu_swap = along(imu_two, "row", swap)
    video_swap = along(video_two, "row", swap)
    return (imu_two, imu_mixed, imu_swap), (video_two, video_mixed, video_swap)


def imu_part(video, video_tags, imu, imu_tags, scale, offset):
    imus, videos = imu_exchange(video, video_tags, imu, imu_tags)
    losses, weighted = weights(video, video_tags, imu, imu_tags, scale, offset)
    loss = row_sum(losses)
    video_grad = to_video(weighted, imu)
    imu_grad = to_partner(weighted, video)
    for other, tags in imus:
        losses, weighted = weights(video, video_tags, other, tags, scale, offset)
        loss = loss + row_sum(losses)
        video_grad = video_grad + to_video(weighted, other)
    for other, tags in videos:
        _, weighted = weights(other, tags, imu, imu_tags, scale, offset)
        imu_grad = imu_grad + to_partner(weighted, other)
    return loss, video_grad, imu_grad


def audio_ring(video, video_tags, audio, audio_tags, scale, offset):
    loss, video_grad, audio_grad = 0.0, 0.0, 0.0
    block, tags = audio, audio_tags
    for rotation in range(STEPS):
        if rotation > 0:
            block, tags = passed_along((block, tags), "col", 1)
            audio_grad = passed_along(audio_grad, "col", 1)
        losses, weighted = weights(video, video_tags, block, tags, scale, offset)
        loss = loss + row_sum(losses)
        video_grad = video_grad + to_video(weighted, block)
        audio_grad = audio_grad + to_partner(weighted, video)
    audio_grad = passed_along(audio_grad, "col", -(STEPS - 1))
    return loss, video_grad, audio_grad


def audio_chain(video, video_tags, audio, audio_tags, scale, offset):
    across = [(1, 2), (2, 1)]
    inward = [(0, 1), (3, 2)]
    outward = [(1, 0), (2, 3)]
    beyond = [(0, 2), (3, 1)]
    step = audio.shape[0] // CHUNKS
    chunks = [slice(k * step, (k + 1) * step) for k in range(CHUNKS)]

    mid, mid_tags = along((audio, audio_tags), "col", across)
    video_out, video_out_tags = along((video, video_tags), "col", inward)
    far, far_tags = along((audio, audio_tags), "col", beyond)
    audio_out, audio_out_tags = along((audio, audio_tags), "col", inward)

    def meet(v, v_tags, a, a_tags):
        losses, weighted = weights(v, v_tags, a, a_tags, scale, offset)
        return row_sum(losses), weighted

    own_loss, own_w = meet(video, video_tags, audio, audio_tags)
    mid_loss, mid_w = meet(video, video_tags, mid, mid_tags)
    far_loss, far_w = meet(video, video_tags, far, far_tags)
    out_loss, out_w = meet(video, video_tags, audio_out, audio_out_tags)
    own_loss_o, own_w_o = meet(video_out, video_out_tags, audio, audio_tags)
    mid_loss_o, mid_w_o = meet(video_out, video_out_tags, mid, mid_tags)
    far_loss_o, far_w_o = meet(video_out, video_out_tags, far, far_tags)

    def sums(w, w_o, rows):
        both = to_partner(w[:, rows], video) + to_partner(w_o[:, rows], video_out)
        return both.astype(jnp.bfloat16)

    mid_sums = [sums(mid_w, mid_w_o, rows) for rows in chunks]
    far_sums = [sums(far_w, far_w_o, rows) for rows in chunks]
    out_own = [to_partner(out_w[:, rows], video) for rows in chunks]

    mid_got = [None] * CHUNKS
    far_got = [None] * CHUNKS
    mid_got[0] = along(mid_sums[0], "col", across)
    for k in range(CHUNKS):
        far_got[k] = along(far_sums[k], "col", across)
    for k in range(1, CHUNKS):
        mid_got[k] = along(mid_sums[k], "col", across)
    video_back = (
        to_video(own_w_o, audio) + to_video(mid_w_o, mid) + to_video(far_w_o, far)
    ).astype(jnp.bfloat16)
    video_got = along(video_back, "col", outward)
    loss_got = along(own_loss_o + mid_loss_o + far_loss_o, "col", outward)
    out_got = [
        along((own + got.astype(jnp.float32)).astype(jnp.bfloat16), "col", outward)
        for own, got in zip(out_own, far_got)
    ]

    place = lax.axis_index("col")
    inner = (place == 1) | (place == 2)
    loss = own_loss + jnp.where(inner, mid_loss + far_loss + out_loss, loss_got)
    video_grad = (
        to_video(own_w, audio)
        + to_video(mid_w, mid)
        + to_video(far_w, far)
        + to_video(out_w, audio_out)
        + video_got.astype(jnp.float32)
    )
    own_grad = to_partner(own_w, video) + to_partner(own_w_o, video_out)
    got = [m.astype(jnp.float32) + o.astype(jnp.float32) for m, o in zip(mid_got, out_got)]
    audio_grad = own_grad + jnp.concatenate(got, axis=0)
    return loss, video_grad, audio_grad


def per_device(
    video_rows,
    video_ids,
    imu_rows,
    imu_ids,
    audio_rows,
    audio_ids,
    imu_log_scale,
    imu_bias,
    audio_log_scale,
    audio_bias,
):
    audio_part = audio_chain if lax.axis_size("col") == STEPS else audio_ring
    audio_loss, audio_video, audio_grad = audio_part(
        video_rows, video_ids, audio_rows, audio_ids, jnp.exp(audio_log_scale[0]), audio_bias[0]
    )
    imu_loss, imu_video, imu_grad = imu_part(
        video_rows, video_ids, imu_rows, imu_ids, jnp.exp(imu_log_scale[0]), imu_bias[0]
    )
    row_loss = (imu_loss + audio_loss) / (2.0 * STEPS * video_rows.shape[0])
    return (imu_video + audio_video, imu_grad, audio_grad, row_loss)


def solution(mesh):
    rows, vector = P(("row", "col"), None), P(("row", "col"))
    return jax.shard_map(
        per_device,
        mesh=mesh,
        in_specs=(rows, vector, rows, vector, rows, vector, P(), P(), P(), P()),
        out_specs=(rows, rows, rows, vector),
        check_vma=False,
    )
```

time: 217 us -> 171 us (0.79)
  waiting for transfers between devices: 177 us -> 39.8 us
  matrix products: 21.5 us -> 82.9 us
  starting transfers between devices: 11.2 us -> 39.2 us
  other arithmetic: 0.59 us -> 3.67 us
    ppermute x20 -> x4, waiting for transfers between devices: 177 us -> 5.26 us  [passed_along(): lax.ppermute(shard, axis, [(i, (i + by) % devices) for i in range(devices)])]
    dot_general x24 -> x38, matrix products: 21.5 us -> 82.9 us  [the longest x11 31.9 us: to_video(): return jnp.dot(weighted, partner, preferred_element_type=jnp.float32)]
    ppermute x0 -> x24, waiting for transfers between devices: none -> 34.5 us  [along(): return lax.ppermute(shard, axis, pairs)]
    ppermute x0 -> x24, starting transfers between devices: none -> 33.1 us  [along(): return lax.ppermute(shard, axis, pairs)]
    ppermute x20 -> x4, starting transfers between devices: 11.2 us -> 6.13 us  [passed_along(): lax.ppermute(shard, axis, [(i, (i + by) % devices) for i in range(devices)])]
    add x0 -> x3, other arithmetic: none -> 3.09 us  [the longest x2 3.08 us: audio_chain(): m.astype(jnp.float32) + o.astype(jnp.float32)]
  transfers between devices with their start and end apart: 20 -> 28, of which waited for: 8 -> 5; matrix products, arithmetic and copies ran while one was open for 10% -> 51% of each run, Pallas kernels for 0% -> 0%
where the time goes in v1:
time: 171 us; the launch traced here: 170 us
  matrix products  82.9 us (48%)
  waiting for transfers between devices  39.8 us (23%)
  starting transfers between devices  39.2 us (23%)
  between operations  3.7 us (2%)
  other arithmetic  3.67 us (2%)
    ppermute x24, waiting for transfers between devices, along(): return lax.ppermute(shard, axis, pairs)  34.5 us
    ppermute x24, starting transfers between devices, along(): return lax.ppermute(shard, axis, pairs)  33.1 us
    dot_general x11, matrix products, to_video(): return jnp.dot(weighted, partner, preferred_element_type=jnp.float32)  31.9 us
    dot_general x16, matrix products, to_partner(): lax.dot_general(weighted, video, (((0,), (0,)), ((), ())), preferred_elem...  31.1 us
    dot_general x11, matrix products, weights(): lax.dot_general(video, partner, (((1,), (1,)), ((), ())), preferred_eleme...  19.9 us
    ppermute x4, starting transfers between devices, passed_along(): lax.ppermute(shard, axis, [(i, (i + by) % devices) for i in range(devices)])  6.13 us
    ppermute x4, waiting for transfers between devices, passed_along(): lax.ppermute(shard, axis, [(i, (i + by) % devices) for i in range(devices)])  5.26 us
  transfers between devices with their start and end apart: 28, of which 5 were waited for; matrix products, arithmetic and copies ran while one was open for 51% of the time, Pallas kernels for 0%

profile of v1, /device:TPU:0, one launch (start us, length us, event | category | flops | bytes accessed | tf_op | source)
XLA Modules:
  0.0 170.2 jit_solution(5305295010557991351)
XLA Ops:
  0.6 6.8 %collective-permute-start.9 = (bf16[384,1024]{1,0:T(8,128)(2,1)}, bf16[384,1024]{1,0:T(8,128)(2,1)}, u32[]{:S(2)}, u32[]{:S(2)}) collective-permute-start(bf16[384,1024]{1,0:T(8,128)(2,1)} %param.14), channel_id=1, source_target_pairs={{0,2},{3,1},{4,6},{7,5},{8,10},{11,9},{12,14},{15,13},{16,18},{19,... | collective-permute-start | bytes 2359304 | tf_op jit(solution)/shard_map/ppermute | solution.py:16
  7.5 0.7 collective-permute-start.7
  8.2 2.2 %collective-permute-start.13 = (bf16[384,1024]{1,0:T(8,128)(2,1)}, bf16[384,1024]{1,0:T(8,128)(2,1)S(1)}, u32[]{:S(2)}, u32[]{:S(2)}) collective-permute-start(bf16[384,1024]{1,0:T(8,128)(2,1)} %param.10), channel_id=1, source_target_pairs={{0,1},{3,2},{4,5},{7,6},{8,9},{11,10},{12,13},{15,14},{16,17},{19,... | collective-permute-start | bytes 2359304 | tf_op jit(solution)/shard_map/ppermute | solution.py:16
  10.4 1.3 collective-permute-start.12
  11.7 1.3 collective-permute-start.8
  14.4 2.4 %fusion.59 = (f32[384]{0:T(512)S(1)}, f32[384,384]{0,1:T(8,128)S(1)}) fusion(f32[]{:T(128)} %bitcast.71, bf16[384,1024]{1,0:T(8,128)(2,1)} %param.10, bf16[384,1024]{1,0:T(8,128)(2,1)} %param.14, f32[]{:T(128)} %bitcast.2, s32[384]{0:T(512)} %param.15, s32[384]{0:T(512)} %param.11), kind=kOutput, calls=%fused_computation.96 | convolution fusion | flops 303906432 | bytes 2167304 | tf_op jit(solution)/shard_map/dot_general | solution.py:20
  16.8 1.9 %fusion.144 = f32[384,1024]{1,0:T(8,128)} fusion(bf16[384,1024]{1,0:T(8,128)(2,1)S(1)} %copy-done, f32[384,384]{0,1:T(8,128)S(1)} %get-tuple-element.15, f32[]{:T(128)} %bitcast.2, s32[384]{0:T(512)S(1)} %copy-done.11, s32[384]{0:T(512)S(1)} %copy-done.15), kind=kOutput, calls=%fused_computation.201 | convolution fusion | flops 303316992 | bytes 2952196 | tf_op jit(solution)/shard_map/dot_general | solution.py:35
  18.6 3.0 %fusion.145 = f32[384,1024]{1,0:T(8,128)} fusion(bf16[384,1024]{1,0:T(8,128)(2,1)} %param.14, f32[384,384]{0,1:T(8,128)S(1)} %get-tuple-element.15, f32[]{:T(128)} %bitcast.2, s32[384]{0:T(512)S(1)} %copy-done.11, s32[384]{0:T(512)S(1)} %copy-done.15), kind=kOutput, calls=%fused_computation.202 | convolution fusion | flops 303316992 | bytes 2952196 | tf_op jit(solution)/shard_map/dot_general | solution.py:31
  23.0 2.1 %fusion.55 = (f32[384]{0:T(512)S(1)}, f32[384,384]{0,1:T(8,128)S(1)}) fusion(f32[]{:T(128)} %bitcast.64, bf16[384,1024]{1,0:T(8,128)(2,1)S(1)} %copy-done, bf16[384,1024]{1,0:T(8,128)(2,1)} %param.12, f32[]{:T(128)} %bitcast, s32[384]{0:T(512)S(1)} %copy-done.12, s32[384]{0:T(512)S(1)} %copy-done.11), kind=kOutput, calls=%fused_computation.92 | convolution fusion | flops 303906432 | bytes 2167304 | tf_op jit(solution)/shard_map/dot_general | solution.py:20
  25.0 3.0 %fusion.143 = f32[384,1024]{1,0:T(8,128)} fusion(bf16[384,1024]{1,0:T(8,128)(2,1)} %param.12, f32[384,384]{0,1:T(8,128)S(1)} %get-tuple-element.23, f32[]{:T(128)} %bitcast, s32[384]{0:T(512)S(1)} %copy-done.11, s32[384]{0:T(512)S(1)} %copy-done.12), kind=kOutput, calls=%fused_computation.200 | convolution fusion | flops 303316992 | bytes 2952196 | tf_op jit(solution)/shard_map/dot_general | solution.py:31
  28.0 2.0 %fusion.142 = f32[384,1024]{1,0:T(8,128)} fusion(bf16[384,1024]{1,0:T(8,128)(2,1)S(1)} %copy-done, f32[384,384]{0,1:T(8,128)S(1)} %get-tuple-element.23, f32[]{:T(128)} %bitcast, s32[384]{0:T(512)S(1)} %copy-done.11, s32[384]{0:T(512)S(1)} %copy-done.12), kind=kOutput, calls=%fused_computation.199 | convolution fusion | flops 303316992 | bytes 2952196 | tf_op jit(solution)/shard_map/dot_general | solution.py:35
  30.0 10.7 %collective-permute-done.12 = s32[384]{0:T(512)S(1)} collective-permute-done((s32[384]{0:T(512)}, s32[384]{0:T(512)S(1)}, u32[]{:S(2)}, u32[]{:S(2)}) %collective-permute-start.12) | collective-permute-done | bytes 1568 | tf_op jit(solution)/shard_map/ppermute | solution.py:16
  40.6 4.3 %collective-permute-start.11 = (bf16[384,1024]{1,0:T(8,128)(2,1)}, bf16[384,1024]{1,0:T(8,128)(2,1)S(1)}, u32[]{:S(2)}, u32[]{:S(2)}) collective-permute-start(bf16[384,1024]{1,0:T(8,128)(2,1)} %param.14), channel_id=1, source_target_pairs={{0,1},{3,2},{4,5},{7,6},{8,9},{11,10},{12,13},{15,14},{16,17},{19,... | collective-permute-start | bytes 2359304 | tf_op jit(solution)/shard_map/ppermute | solution.py:16
  45.7 2.1 %fusion.63 = (f32[384]{0:T(512)S(1)}, f32[384,384]{0,1:T(8,128)S(1)}) fusion(f32[]{:T(128)} %bitcast.74, bf16[384,1024]{1,0:T(8,128)(2,1)S(1)} %collective-permute-done.13, bf16[384,1024]{1,0:T(8,128)(2,1)} %param.14, f32[]{:T(128)} %bitcast.2, s32[384]{0:T(512)S(1)} %copy-done.15, s32[384]{0:T(512)S(1)} %collective-permute-done.12), kind=kOutput, calls=%fused_computation.100 | convolution fusion | flops 303906432 | bytes 2167304 | tf_op jit(solution)/shard_map/dot_general | solution.py:20
  47.7 3.2 %fusion.146 = f32[384,1024]{1,0:T(8,128)} fusion(bf16[384,1024]{1,0:T(8,128)(2,1)} %param.14, f32[384,384]{0,1:T(8,128)S(1)} %get-tuple-element.17, s32[384]{0:T(512)S(1)} %collective-permute-done.12, f32[]{:T(128)} %bitcast.2, s32[384]{0:T(512)S(1)} %copy-done.15), kind=kOutput, calls=%fused_computation.203 | convolution fusion | flops 303316992 | bytes 2952196 | tf_op jit(solution)/shard_map/dot_general | solution.py:31
  50.9 2.9 %collective-permute-start.10 = (s32[384]{0:T(512)S(1)}, s32[384]{0:T(512)S(1)}, u32[]{:S(2)}, u32[]{:S(2)}) collective-permute-start(s32[384]{0:T(512)S(1)} %copy-done.15), channel_id=1, source_target_pairs={{0,1},{3,2},{4,5},{7,6},{8,9},{11,10},{12,13},{15,14},{16,17},{19,... | collective-permute-start | bytes 4616 | tf_op jit(solution)/shard_map/ppermute | solution.py:16
  53.9 1.5 collective-permute-start.1
  55.4 1.1 fusion.64
  56.5 1.7 %fusion.150 = f32[384,1024]{1,0:T(8,128)} fusion(bf16[384,384]{0,1:T(8,128)(2,1)S(1)} %get-tuple-element.11, bf16[384,1024]{1,0:T(8,128)(2,1)S(1)} %collective-permute-done.7), kind=kOutput, calls=%fused_computation.207 | convolution fusion | flops 301989888 | bytes 2654208 | tf_op jit(solution)/shard_map/dot_general | solution.py:31
  58.2 1.1 fusion.60
  59.3 1.8 %fusion.147 = f32[384,1024]{1,0:T(8,128)S(1)} fusion(bf16[384,384]{0,1:T(8,128)(2,1)S(1)} %get-tuple-element.7, bf16[384,1024]{1,0:T(8,128)(2,1)} %copy-done.2), kind=kOutput, calls=%fused_computation.204 | convolution fusion | flops 301989888 | bytes 2654208 | tf_op jit(solution)/shard_map/dot_general | solution.py:31
  61.1 1.6 collective-permute-start
  62.7 2.2 %fusion.61 = (f32[384]{0:T(512)S(1)}, bf16[384,384]{0,1:T(8,128)(2,1)S(1)}) fusion(f32[]{:T(128)} %bitcast.2, s32[384]{0:T(512)S(1)} %collective-permute-done.8, s32[384]{0:T(512)S(1)} %copy-done.11, f32[]{:T(128)} %bitcast.76, bf16[384,1024]{1,0:T(8,128)(2,1)S(1)} %copy-done, bf16[384,1024]{1,0:T(8,128)(2,1)} %collective-permute-done.9), kind=kOutput, calls=%fused_computation.98 | convolution fusion | flops 304791168 | bytes 1872392 | tf_op jit(solution)/shard_map/dot_general | solution.py:20
  64.9 2.9 %fusion.148 = f32[384,1024]{1,0:T(8,128)} fusion(bf16[384,384]{0,1:T(8,128)(2,1)S(1)} %get-tuple-element.5, bf16[384,1024]{1,0:T(8,128)(2,1)} %collective-permute-done.9), kind=kOutput, calls=%fused_computation.205 | convolution fusion | flops 301989888 | bytes 2654208 | tf_op jit(solution)/shard_map/dot_general | solution.py:31
  67.8 5.3 %collective-permute-done = s32[384]{0:T(512)S(1)} collective-permute-done((s32[384]{0:T(512)S(1)}, s32[384]{0:T(512)S(1)}, u32[]{:S(2)}, u32[]{:S(2)}) %collective-permute-start) | collective-permute-done | bytes 1568 | tf_op jit(solution)/shard_map/ppermute | solution.py:12
  73.1 1.5 collective-permute-start.16
  74.5 2.1 %fusion.56 = (f32[384]{0:T(512)S(1)}, f32[384,384]{0,1:T(8,128)S(1)}) fusion(f32[]{:T(128)} %bitcast.70, bf16[384,1024]{1,0:T(8,128)(2,1)S(1)} %copy-done, bf16[384,1024]{1,0:T(8,128)(2,1)} %collective-permute-done.1, f32[]{:T(128)} %bitcast, s32[384]{0:T(512)S(1)} %collective-permute-done, s32[384]{0:T(512)S(1)} %copy-done.11), kind=kOutput, calls=%fused_computation.93 | convolution fusion | flops 303906432 | bytes 2167304 | tf_op jit(solution)/shard_map/dot_general | solution.py:20
  76.6 3.0 %fusion.75 = f32[384,1024]{1,0:T(8,128)} fusion(bf16[384,1024]{1,0:T(8,128)(2,1)} %collective-permute-done.1, f32[384,384]{0,1:T(8,128)S(1)} %get-tuple-element.25, f32[]{:T(128)} %bitcast, s32[384]{0:T(512)S(1)} %copy-done.11, s32[384]{0:T(512)S(1)} %collective-permute-done), kind=kOutput, calls=%fused_computation.134 | convolution fusion | flops 303316992 | bytes 2952196 | tf_op jit(solution)/shard_map/dot_general | solution.py:31
  80.0 1.6 collective-permute-start.15
  81.5 1.2 collective-permute-start.18
  82.7 1.1 fusion.62
  83.8 1.7 %fusion.149 = f32[384,1024]{1,0:T(8,128)} fusion(bf16[384,384]{0,1:T(8,128)(2,1)S(1)} %get-tuple-element.9, bf16[384,1024]{1,0:T(8,128)(2,1)S(1)} %collective-permute-done.11), kind=kOutput, calls=%fused_computation.206 | convolution fusion | flops 301989888 | bytes 2654208 | tf_op jit(solution)/shard_map/dot_general | solution.py:31
  85.6 1.1 fusion.2
  86.7 2.2 %fusion.65 = (f32[384]{0:T(512)S(1)}, bf16[384,384]{0,1:T(8,128)(2,1)S(1)}) fusion(f32[]{:T(128)} %bitcast.2, s32[384]{0:T(512)S(1)} %collective-permute-done.8, s32[384]{0:T(512)S(1)} %collective-permute-done.12, f32[]{:T(128)} %bitcast.72, bf16[384,1024]{1,0:T(8,128)(2,1)S(1)} %collective-permute-done.13, bf16[384,1024]{1,0:T(8,128)(2,1)} %collective-permute-done.9), kind=kOutput, calls=%fused_computation.102 | convolution fusion | flops 304791168 | bytes 1872392 | tf_op jit(solution)/shard_map/dot_general | solution.py:20
  89.8 0.9 fusion.57
  90.8 1.1 fusion.3
  91.9 1.8 %fusion.76 = f32[384,1024]{1,0:T(8,128)} fusion(bf16[384,1024]{1,0:T(8,128)(2,1)S(1)} %collective-permute-done.3, f32[384,384]{0,1:T(8,128)S(1)} %get-tuple-element.21, f32[]{:T(128)} %bitcast, s32[384]{0:T(512)S(1)} %copy-done.11, s32[384]{0:T(512)S(1)} %collective-permute-done.2), kind=kOutput, calls=%fused_computation.135 | convolution fusion | flops 303316992 | bytes 2952196 | tf_op jit(solution)/shard_map/dot_general | solution.py:31
  93.7 1.3 fusion.121
  95.0 1.4 collective-permute-start.25
  96.4 0.9 copy-done.13
  97.3 1.4 collective-permute-start.24
  98.7 4.0 %fusion.53 = f32[384,1024]{1,0:T(8,128)} fusion(bf16[384,1024]{1,0:T(8,128)(2,1)} %copy-done.13, bf16[384,1024]{1,0:T(8,128)(2,1)} %param.12, s32[384]{0:T(512)S(1)} %collective-permute-done.15, f32[]{:T(128)} %bitcast.67, f32[]{:T(128)} %bitcast, s32[384]{0:T(512)S(1)} %copy-done.12), kind=kOutput, calls=%fused_computation.86 | convolution fusion | flops 605749248 | bytes 3148808 | tf_op jit(solution)/shard_map/dot_general | solution.py:35
  102.7 2.4 %fusion.1 = bf16[192,1024]{1,0:T(8,128)(2,1)} fusion(f32[192,1024]{1,0:T(8,128)} %fusion.121, bf16[384,1024]{1,0:T(8,128)(2,1)S(1)} %collective-permute-done.13, bf16[384,384]{0,1:T(8,128)(2,1)S(1)} %get-tuple-element.13), kind=kOutput, calls=%fused_computation.20 | convolution fusion | flops 151388160 | bytes 2113536 | tf_op jit(solution)/shard_map/dot_general | solution.py:35
  105.1 3.2 %add_convert_fusion = bf16[384,1024]{1,0:T(8,128)(2,1)} fusion(f32[384,1024]{1,0:T(8,128)} %fusion.146, f32[384,1024]{1,0:T(8,128)S(1)} %copy-done.1, bf16[384,384]{0,1:T(8,128)(2,1)S(1)} %get-tuple-element.13, bf16[384,1024]{1,0:T(8,128)(2,1)} %collective-permute-done.9), kind=kOutput, calls=%fused_computation.14 | convolution fusion | flops 303169536 | bytes 5013504 | tf_op jit(solution)/shard_map/dot_general | solution.py:31
  108.3 1.3 fusion.128
  109.5 1.4 collective-permute-start.22
  111.0 4.0 %fusion.54 = f32[384,1024]{1,0:T(8,128)} fusion(bf16[384,1024]{1,0:T(8,128)(2,1)} %collective-permute-done.18, bf16[384,1024]{1,0:T(8,128)(2,1)} %param.12, s32[384]{0:T(512)S(1)} %collective-permute-done.17, f32[]{:T(128)} %bitcast.66, f32[]{:T(128)} %bitcast, s32[384]{0:T(512)S(1)} %copy-done.12), kind=kOutput, calls=%fused_computation.87 | convolution fusion | flops 605749248 | bytes 3148808 | tf_op jit(solution)/shard_map/dot_general | solution.py:35
  115.0 1.6 fusion
  116.6 0.8 collective-permute-start.21
  117.4 1.4 add_convert_fusion.1
  118.8 1.3 collective-permute-start.26
  120.1 1.4 add_convert_fusion.2
  122.0 1.5 collective-permute-start.23
  123.5 2.9 %fusion.58 = (f32[384]{0:T(512)S(1)}, f32[384,384]{0,1:T(8,128)}) fusion(f32[]{:T(128)} %bitcast.68, bf16[384,1024]{1,0:T(8,128)(2,1)S(1)} %copy-done, bf16[384,1024]{1,0:T(8,128)(2,1)} %collective-permute-done.5, f32[]{:T(128)} %bitcast, s32[384]{0:T(512)S(1)} %collective-permute-done.4, s32[384]{0:T(512)S(1)} %copy-done.11), kind=kOutput, calls=%fused_computation.95 | convolution fusion | flops 303906432 | bytes 2167304 | tf_op jit(solution)/shard_map/dot_general | solution.py:20
  126.4 10.0 %collective-permute-done.26 = bf16[192,1024]{1,0:T(8,128)(2,1)S(1)} collective-permute-done((bf16[192,1024]{1,0:T(8,128)(2,1)S(1)}, bf16[192,1024]{1,0:T(8,128)(2,1)S(1)}, u32[]{:S(2)}, u32[]{:S(2)}) %collective-permute-start.26) | collective-permute-done | bytes 393248 | tf_op jit(solution)/shard_map/ppermute | solution.py:16
  136.4 1.3 collective-permute-start.14
  137.7 2.1 %convert_add_fusion = f32[192,1024]{1,0:T(8,128)} fusion(bf16[192,1024]{1,0:T(8,128)(2,1)S(1)} %collective-permute-done.26, bf16[192,1024]{1,0:T(8,128)(2,1)} %collective-permute-done.24), kind=kLoop, calls=%fused_computation.88 | loop fusion | flops 589824 | bytes 1572864 | tf_op jit(solution)/shard_map/add | solution.py:152
  139.8 1.3 collective-permute-start.27
  141.1 3.8 %collective-permute-done.23 = bf16[192,1024]{1,0:T(8,128)(2,1)S(1)} collective-permute-done((bf16[192,1024]{1,0:T(8,128)(2,1)S(1)}, bf16[192,1024]{1,0:T(8,128)(2,1)S(1)}, u32[]{:S(2)}, u32[]{:S(2)}) %collective-permute-start.23) | collective-permute-done | bytes 393248 | tf_op jit(solution)/shard_map/ppermute | solution.py:16
  144.8 1.0 convert_add_fusion.1
  145.9 5.4 %add_add_fusion = f32[384,1024]{1,0:T(8,128)} fusion(f32[384,1024]{1,0:T(8,128)} %fusion.54, f32[384,1024]{1,0:T(8,128)} %fusion.142, f32[384,1024]{1,0:T(8,128)} %fusion.53, bf16[384,1024]{1,0:T(8,128)(2,1)} %collective-permute-done.20, bf16[384,1024]{1,0:T(8,128)(2,1)} %param.12, s32[384]{0:T(512)S(1)} %collective-permute-done.19, f32[]{:T(128)} %bitcast.65, ...), kind=kOutput, calls=%fused_computation.12 | convolution fusion | flops 606928896 | bytes 7867400 | tf_op jit(solution)/shard_map/dot_general | solution.py:35
  151.3 10.1 %collective-permute-done.14 = bf16[384,1024]{1,0:T(8,128)(2,1)S(1)} collective-permute-done((bf16[384,1024]{1,0:T(8,128)(2,1)}, bf16[384,1024]{1,0:T(8,128)(2,1)S(1)}, u32[]{:S(2)}, u32[]{:S(2)}) %collective-permute-start.14) | collective-permute-done | bytes 786464 | tf_op jit(solution)/shard_map/ppermute | solution.py:16
  161.3 6.4 %add_add_fusion.1 = f32[384,1024]{1,0:T(8,128)} fusion(bf16[384,1024]{1,0:T(8,128)(2,1)S(1)} %collective-permute-done.14, f32[384,1024]{1,0:T(8,128)} %fusion.149, f32[384,1024]{1,0:T(8,128)} %fusion.148, f32[384,1024]{1,0:T(8,128)} %fusion.145, f32[384,1024]{1,0:T(8,128)S(1)} %fusion.147, f32[384,1024]{1,0:T(8,128)} %fusion.76, f32[384,1024]{1,0:T(8,128)} %fusion.143, ...), kind=kOutput, calls=%fused_computation.13 | convolution fusion | flops 306855936 | bytes 14748676 | tf_op jit(solution)/shard_map/dot_general | solution.py:31
  167.8 1.8 %maximum_add_fusion = f32[384,1024]{1,0:T(8,128)} fusion(f32[192,1024]{1,0:T(8,128)S(1)} %copy-done.9, f32[192,1024]{1,0:T(8,128)S(1)} %copy-done.10, f32[384,1024]{1,0:T(8,128)S(1)} %copy-done.16, bf16[384,1024]{1,0:T(8,128)(2,1)S(1)} %collective-permute-done.13, f32[384,384]{0,1:T(8,128)S(1)} %copy-done.18, s32[384]{0:T(512)S(1)} %collective-permute-done.12, ...), kind=kOutput, calls=%fused_computation.11 | convolution fusion | flops 304496640 | bytes 6097924 | tf_op jit(solution)/shard_map/dot_general | solution.py:35
  (72 shorter events, 3.3 us)
Async XLA Ops:
  0.6 62.1 %collective-permute-start.9 = (bf16[384,1024]{1,0:T(8,128)(2,1)}, bf16[384,1024]{1,0:T(8,128)(2,1)}, u32[]{:S(2)}, u32[]{:S(2)}) collective-permute-start(bf16[384,1024]{1,0:T(8,128)(2,1)} %param.14), channel_id=1, source_target_pairs={{0,2},{3,1},{4,6},{7,5},{8,10},{11,9},{12,14},{15,13},{16,18},{19,... | collective-permute-start | bytes 2359304 | tf_op jit(solution)/shard_map/ppermute | solution.py:16
  7.5 46.4 %collective-permute-start.7 = (bf16[384,1024]{1,0:T(8,128)(2,1)}, bf16[384,1024]{1,0:T(8,128)(2,1)S(1)}, u32[]{:S(2)}, u32[]{:S(2)}) collective-permute-start(bf16[384,1024]{1,0:T(8,128)(2,1)} %param.14), channel_id=1, source_target_pairs={{1,2},{2,1},{5,6},{6,5},{9,10},{10,9},{13,14},{14,13},{17,18},{18,... | collective-permute-start | bytes 2359304 | tf_op jit(solution)/shard_map/ppermute | solution.py:16
  8.2 36.8 %collective-permute-start.13 = (bf16[384,1024]{1,0:T(8,128)(2,1)}, bf16[384,1024]{1,0:T(8,128)(2,1)S(1)}, u32[]{:S(2)}, u32[]{:S(2)}) collective-permute-start(bf16[384,1024]{1,0:T(8,128)(2,1)} %param.10), channel_id=1, source_target_pairs={{0,1},{3,2},{4,5},{7,6},{8,9},{11,10},{12,13},{15,14},{16,17},{19,... | collective-permute-start | bytes 2359304 | tf_op jit(solution)/shard_map/ppermute | solution.py:16
  10.4 30.2 %collective-permute-start.12 = (s32[384]{0:T(512)}, s32[384]{0:T(512)S(1)}, u32[]{:S(2)}, u32[]{:S(2)}) collective-permute-start(s32[384]{0:T(512)} %param.11), channel_id=1, source_target_pairs={{0,1},{3,2},{4,5},{7,6},{8,9},{11,10},{12,13},{15,14},{16,17},{19,... | collective-permute-start | bytes 4616 | tf_op jit(solution)/shard_map/ppermute | solution.py:16
  11.7 49.4 %collective-permute-start.8 = (s32[384]{0:T(512)}, s32[384]{0:T(512)S(1)}, u32[]{:S(2)}, u32[]{:S(2)}) collective-permute-start(s32[384]{0:T(512)} %param.15), channel_id=1, source_target_pairs={{0,2},{3,1},{4,6},{7,5},{8,10},{11,9},{12,14},{15,13},{16,18},{19,... | collective-permute-start | bytes 4616 | tf_op jit(solution)/shard_map/ppermute | solution.py:16
  14.3 2.4 %copy-start = (bf16[384,1024]{1,0:T(8,128)(2,1)S(1)}, bf16[384,1024]{1,0:T(8,128)(2,1)}, u32[]{:S(2)}) copy-start(bf16[384,1024]{1,0:T(8,128)(2,1)} %param.10) | copy-start | bytes 2359300
  14.3 2.4 %copy-start.11 = (s32[384]{0:T(512)S(1)}, s32[384]{0:T(512)}, u32[]{:S(2)}) copy-start(s32[384]{0:T(512)} %param.11) | copy-start | bytes 4612
  14.4 2.4 %copy-start.15 = (s32[384]{0:T(512)S(1)}, s32[384]{0:T(512)}, u32[]{:S(2)}) copy-start(s32[384]{0:T(512)} %param.15) | copy-start | bytes 4612
  18.6 4.3 %copy-start.12 = (s32[384]{0:T(512)S(1)}, s32[384]{0:T(512)}, u32[]{:S(2)}) copy-start(s32[384]{0:T(512)} %param.13) | copy-start | bytes 4612
  40.6 40.9 %collective-permute-start.11 = (bf16[384,1024]{1,0:T(8,128)(2,1)}, bf16[384,1024]{1,0:T(8,128)(2,1)S(1)}, u32[]{:S(2)}, u32[]{:S(2)}) collective-permute-start(bf16[384,1024]{1,0:T(8,128)(2,1)} %param.14), channel_id=1, source_target_pairs={{0,1},{3,2},{4,5},{7,6},{8,9},{11,10},{12,13},{15,14},{16,17},{19,... | collective-permute-start | bytes 2359304 | tf_op jit(solution)/shard_map/ppermute | solution.py:16
  45.0 5.9 %collective-permute-start.6 = (s32[384]{0:T(512)S(1)}, s32[384]{0:T(512)S(1)}, u32[]{:S(2)}, u32[]{:S(2)}) collective-permute-start(s32[384]{0:T(512)S(1)} %copy-done.15), channel_id=1, source_target_pairs={{1,2},{2,1},{5,6},{6,5},{9,10},{10,9},{13,14},{14,13},{17,18},{18,... | collective-permute-start | bytes 4616 | tf_op jit(solution)/shard_map/ppermute | solution.py:16
  47.7 3.2 %copy-start.17 = (f32[384,384]{0,1:T(8,128)}, f32[384,384]{0,1:T(8,128)S(1)}, u32[]{:S(2)}) copy-start(f32[384,384]{0,1:T(8,128)S(1)} %get-tuple-element.17) | copy-start | bytes 1769476
  50.9 29.0 %collective-permute-start.10 = (s32[384]{0:T(512)S(1)}, s32[384]{0:T(512)S(1)}, u32[]{:S(2)}, u32[]{:S(2)}) collective-permute-start(s32[384]{0:T(512)S(1)} %copy-done.15), channel_id=1, source_target_pairs={{0,1},{3,2},{4,5},{7,6},{8,9},{11,10},{12,13},{15,14},{16,17},{19,... | collective-permute-start | bytes 4616 | tf_op jit(solution)/shard_map/ppermute | solution.py:16
  53.9 4.4 %copy-start.2 = (bf16[384,1024]{1,0:T(8,128)(2,1)}, bf16[384,1024]{1,0:T(8,128)(2,1)S(1)}, u32[]{:S(2)}) copy-start(bf16[384,1024]{1,0:T(8,128)(2,1)S(1)} %collective-permute-done.7) | copy-start | bytes 2359300
  53.9 19.2 %collective-permute-start.1 = (bf16[384,1024]{1,0:T(8,128)(2,1)}, bf16[384,1024]{1,0:T(8,128)(2,1)}, u32[]{:S(2)}, u32[]{:S(2)}) collective-permute-start(bf16[384,1024]{1,0:T(8,128)(2,1)} %param.12), channel_id=1, source_target_pairs={{0,8},{4,12},{8,16},{12,20},{16,24},{20,28},{24,0},{28,4},{1,9},{5... | collective-permute-start | bytes 2359304 | tf_op jit(solution)/shard_map/ppermute | solution.py:12
  56.5 29.1 %copy-start.3 = (bf16[384,384]{0,1:T(8,128)(2,1)}, bf16[384,384]{0,1:T(8,128)(2,1)S(1)}, u32[]{:S(2)}) copy-start(bf16[384,384]{0,1:T(8,128)(2,1)S(1)} %get-tuple-element.11) | copy-start | bytes 884740
  59.3 20.3 %copy-start.5 = (bf16[384,384]{0,1:T(8,128)(2,1)}, bf16[384,384]{0,1:T(8,128)(2,1)S(1)}, u32[]{:S(2)}) copy-start(bf16[384,384]{0,1:T(8,128)(2,1)S(1)} %get-tuple-element.7) | copy-start | bytes 884740
  61.1 11.9 %collective-permute-start = (s32[384]{0:T(512)S(1)}, s32[384]{0:T(512)S(1)}, u32[]{:S(2)}, u32[]{:S(2)}) collective-permute-start(s32[384]{0:T(512)S(1)} %copy-done.12), channel_id=1, source_target_pairs={{0,8},{4,12},{8,16},{12,20},{16,24},{20,28},{24,0},{28,4},{1,9},{5... | collective-permute-start | bytes 4616 | tf_op jit(solution)/shard_map/ppermute | solution.py:12
  62.7 26.6 %collective-permute-start.3 = (bf16[384,1024]{1,0:T(8,128)(2,1)}, bf16[384,1024]{1,0:T(8,128)(2,1)S(1)}, u32[]{:S(2)}, u32[]{:S(2)}) collective-permute-start(bf16[384,1024]{1,0:T(8,128)(2,1)} %param.12), channel_id=1, source_target_pairs={{0,4},{4,16},{8,12},{12,24},{16,20},{20,0},{24,28},{28,8},{1,5},{5... | collective-permute-start | bytes 2359304 | tf_op jit(solution)/shard_map/ppermute | solution.py:16
  73.1 16.2 %collective-permute-start.2 = (s32[384]{0:T(512)S(1)}, s32[384]{0:T(512)S(1)}, u32[]{:S(2)}, u32[]{:S(2)}) collective-permute-start(s32[384]{0:T(512)S(1)} %copy-done.12), channel_id=1, source_target_pairs={{0,4},{4,16},{8,12},{12,24},{16,20},{20,0},{24,28},{28,8},{1,5},{5... | collective-permute-start | bytes 4616 | tf_op jit(solution)/shard_map/ppermute | solution.py:16
  73.1 23.3 %collective-permute-start.16 = (bf16[384,1024]{1,0:T(8,128)(2,1)S(1)}, bf16[384,1024]{1,0:T(8,128)(2,1)S(1)}, u32[]{:S(2)}, u32[]{:S(2)}) collective-permute-start(bf16[384,1024]{1,0:T(8,128)(2,1)S(1)} %copy-done), channel_id=1, source_target_pairs={{0,24},{4,28},{8,0},{12,4},{16,8},{20,12},{24,16},{28,20},{1,25},{... | collective-permute-start | bytes 2359304 | tf_op jit(solution)/shard_map/ppermute | solution.py:12
  80.0 15.0 %collective-permute-start.15 = (s32[384]{0:T(512)S(1)}, s32[384]{0:T(512)S(1)}, u32[]{:S(2)}, u32[]{:S(2)}) collective-permute-start(s32[384]{0:T(512)S(1)} %copy-done.11), channel_id=1, source_target_pairs={{0,24},{4,28},{8,0},{12,4},{16,8},{20,12},{24,16},{28,20},{1,25},{... | collective-permute-start | bytes 4616 | tf_op jit(solution)/shard_map/ppermute | solution.py:12
  81.5 29.4 %collective-permute-start.18 = (bf16[384,1024]{1,0:T(8,128)(2,1)S(1)}, bf16[384,1024]{1,0:T(8,128)(2,1)}, u32[]{:S(2)}, u32[]{:S(2)}) collective-permute-start(bf16[384,1024]{1,0:T(8,128)(2,1)S(1)} %copy-done), channel_id=1, source_target_pairs={{0,20},{4,0},{8,28},{12,8},{16,4},{20,16},{24,12},{28,24},{1,21},{... | collective-permute-start | bytes 2359304 | tf_op jit(solution)/shard_map/ppermute | solution.py:16
  83.8 2.9 %copy-start.7 = (bf16[384,384]{0,1:T(8,128)(2,1)}, bf16[384,384]{0,1:T(8,128)(2,1)S(1)}, u32[]{:S(2)}) copy-start(bf16[384,384]{0,1:T(8,128)(2,1)S(1)} %get-tuple-element.9) | copy-start | bytes 884740
  89.3 20.3 %collective-permute-start.17 = (s32[384]{0:T(512)S(1)}, s32[384]{0:T(512)S(1)}, u32[]{:S(2)}, u32[]{:S(2)}) collective-permute-start(s32[384]{0:T(512)S(1)} %copy-done.11), channel_id=1, source_target_pairs={{0,20},{4,0},{8,28},{12,8},{16,4},{20,16},{24,12},{28,24},{1,21},{... | collective-permute-start | bytes 4616 | tf_op jit(solution)/shard_map/ppermute | solution.py:16
  89.4 32.1 %collective-permute-start.4 = (s32[384]{0:T(512)S(1)}, s32[384]{0:T(512)S(1)}, u32[]{:S(2)}, u32[]{:S(2)}) collective-permute-start(s32[384]{0:T(512)S(1)} %collective-permute-done), channel_id=1, source_target_pairs={{0,4},{4,0},{8,12},{12,8},{16,20},{20,16},{24,28},{28,24},{1,5},{5... | collective-permute-start | bytes 4616 | tf_op jit(solution)/shard_map/ppermute | solution.py:16
  95.0 21.6 %collective-permute-start.25 = (bf16[192,1024]{1,0:T(8,128)(2,1)}, bf16[192,1024]{1,0:T(8,128)(2,1)}, u32[]{:S(2)}, u32[]{:S(2)}) collective-permute-start(bf16[192,1024]{1,0:T(8,128)(2,1)} %fusion.3), channel_id=1, source_target_pairs={{1,2},{2,1},{5,6},{6,5},{9,10},{10,9},{13,14},{14,13},{17,18},{18,... | collective-permute-start | bytes 1179656 | tf_op jit(solution)/shard_map/ppermute | solution.py:16
  96.4 0.9 copy-start.13
  97.3 29.1 %collective-permute-start.24 = (bf16[192,1024]{1,0:T(8,128)(2,1)}, bf16[192,1024]{1,0:T(8,128)(2,1)}, u32[]{:S(2)}, u32[]{:S(2)}) collective-permute-start(bf16[192,1024]{1,0:T(8,128)(2,1)} %fusion.2), channel_id=1, source_target_pairs={{1,2},{2,1},{5,6},{6,5},{9,10},{10,9},{13,14},{14,13},{17,18},{18,... | collective-permute-start | bytes 1179656 | tf_op jit(solution)/shard_map/ppermute | solution.py:16
  102.7 2.4 %copy-start.1 = (f32[384,1024]{1,0:T(8,128)S(1)}, f32[384,1024]{1,0:T(8,128)}, u32[]{:S(2)}) copy-start(f32[384,1024]{1,0:T(8,128)} %fusion.150) | copy-start | bytes 4718596
  105.1 3.2 %copy-start.6 = (bf16[384,384]{0,1:T(8,128)(2,1)S(1)}, bf16[384,384]{0,1:T(8,128)(2,1)}, u32[]{:S(2)}) copy-start(bf16[384,384]{0,1:T(8,128)(2,1)} %copy-done.5) | copy-start | bytes 884740
  109.5 9.3 %collective-permute-start.22 = (bf16[192,1024]{1,0:T(8,128)(2,1)}, bf16[192,1024]{1,0:T(8,128)(2,1)}, u32[]{:S(2)}, u32[]{:S(2)}) collective-permute-start(bf16[192,1024]{1,0:T(8,128)(2,1)} %fusion.1), channel_id=1, source_target_pairs={{1,2},{2,1},{5,6},{6,5},{9,10},{10,9},{13,14},{14,13},{17,18},{18,... | collective-permute-start | bytes 1179656 | tf_op jit(solution)/shard_map/ppermute | solution.py:16
  111.0 11.0 %collective-permute-start.5 = (bf16[384,1024]{1,0:T(8,128)(2,1)}, bf16[384,1024]{1,0:T(8,128)(2,1)}, u32[]{:S(2)}, u32[]{:S(2)}) collective-permute-start(bf16[384,1024]{1,0:T(8,128)(2,1)} %collective-permute-done.1), channel_id=1, source_target_pairs={{0,4},{4,0},{8,12},{12,8},{16,20},{20,16},{24,28},{28,24},{1,5},{5... | collective-permute-start | bytes 2359304 | tf_op jit(solution)/shard_map/ppermute | solution.py:16
  111.0 4.0 %copy-start.4 = (bf16[384,384]{0,1:T(8,128)(2,1)S(1)}, bf16[384,384]{0,1:T(8,128)(2,1)}, u32[]{:S(2)}) copy-start(bf16[384,384]{0,1:T(8,128)(2,1)} %copy-done.3) | copy-start | bytes 884740
  115.0 2.4 %copy-start.8 = (bf16[384,384]{0,1:T(8,128)(2,1)S(1)}, bf16[384,384]{0,1:T(8,128)(2,1)}, u32[]{:S(2)}) copy-start(bf16[384,384]{0,1:T(8,128)(2,1)} %copy-done.7) | copy-start | bytes 884740
  116.6 4.9 %copy-start.14 = (bf16[384,1024]{1,0:T(8,128)(2,1)S(1)}, bf16[384,1024]{1,0:T(8,128)(2,1)}, u32[]{:S(2)}) copy-start(bf16[384,1024]{1,0:T(8,128)(2,1)} %copy-done.13) | copy-start | bytes 2359300
  116.6 23.2 %collective-permute-start.21 = (bf16[192,1024]{1,0:T(8,128)(2,1)S(1)}, bf16[192,1024]{1,0:T(8,128)(2,1)S(1)}, u32[]{:S(2)}, u32[]{:S(2)}) collective-permute-start(bf16[192,1024]{1,0:T(8,128)(2,1)S(1)} %fusion), channel_id=1, source_target_pairs={{1,2},{2,1},{5,6},{6,5},{9,10},{10,9},{13,14},{14,13},{17,18},{18,... | collective-permute-start | bytes 1179656 | tf_op jit(solution)/shard_map/ppermute | solution.py:16
  118.8 17.6 %collective-permute-start.26 = (bf16[192,1024]{1,0:T(8,128)(2,1)S(1)}, bf16[192,1024]{1,0:T(8,128)(2,1)S(1)}, u32[]{:S(2)}, u32[]{:S(2)}) collective-permute-start(bf16[192,1024]{1,0:T(8,128)(2,1)S(1)} %add_convert_fusion.1), channel_id=1, source_target_pairs={{1,0},{2,3},{5,4},{6,7},{9,8},{10,11},{13,12},{14,15},{17,16},{18,... | collective-permute-start | bytes 1179656 | tf_op jit(solution)/shard_map/ppermute | solution.py:16
  121.5 24.4 %collective-permute-start.20 = (bf16[384,1024]{1,0:T(8,128)(2,1)S(1)}, bf16[384,1024]{1,0:T(8,128)(2,1)}, u32[]{:S(2)}, u32[]{:S(2)}) collective-permute-start(bf16[384,1024]{1,0:T(8,128)(2,1)S(1)} %copy-done.14), channel_id=1, source_target_pairs={{0,4},{4,0},{8,12},{12,8},{16,20},{20,16},{24,28},{28,24},{1,5},{5... | collective-permute-start | bytes 2359304 | tf_op jit(solution)/shard_map/ppermute | solution.py:16
  122.0 22.8 %collective-permute-start.23 = (bf16[192,1024]{1,0:T(8,128)(2,1)S(1)}, bf16[192,1024]{1,0:T(8,128)(2,1)S(1)}, u32[]{:S(2)}, u32[]{:S(2)}) collective-permute-start(bf16[192,1024]{1,0:T(8,128)(2,1)S(1)} %add_convert_fusion.2), channel_id=1, source_target_pairs={{1,0},{2,3},{5,4},{6,7},{9,8},{10,11},{13,12},{14,15},{17,16},{18,... | collective-permute-start | bytes 1179656 | tf_op jit(solution)/shard_map/ppermute | solution.py:16
  126.4 19.5 %collective-permute-start.19 = (s32[384]{0:T(512)S(1)}, s32[384]{0:T(512)S(1)}, u32[]{:S(2)}, u32[]{:S(2)}) collective-permute-start(s32[384]{0:T(512)S(1)} %collective-permute-done.15), channel_id=1, source_target_pairs={{0,4},{4,0},{8,12},{12,8},{16,20},{20,16},{24,28},{28,24},{1,5},{5... | collective-permute-start | bytes 4616 | tf_op jit(solution)/shard_map/ppermute | solution.py:16
  136.4 24.9 %collective-permute-start.14 = (bf16[384,1024]{1,0:T(8,128)(2,1)}, bf16[384,1024]{1,0:T(8,128)(2,1)S(1)}, u32[]{:S(2)}, u32[]{:S(2)}) collective-permute-start(bf16[384,1024]{1,0:T(8,128)(2,1)} %add_convert_fusion), channel_id=1, source_target_pairs={{1,0},{2,3},{5,4},{6,7},{9,8},{10,11},{13,12},{14,15},{17,16},{18,... | collective-permute-start | bytes 2359304 | tf_op jit(solution)/shard_map/ppermute | solution.py:16
  139.8 29.9 %collective-permute-start.27 = (f32[384]{0:T(512)S(1)}, f32[384]{0:T(512)S(1)}, u32[]{:S(2)}, u32[]{:S(2)}) collective-permute-start(f32[384]{0:T(512)S(1)} %add_add_fusion.2), channel_id=1, source_target_pairs={{1,0},{2,3},{5,4},{6,7},{9,8},{10,11},{13,12},{14,15},{17,16},{18,... | collective-permute-start | bytes 4616 | tf_op jit(solution)/shard_map/ppermute | solution.py:16
  161.3 6.4 %copy-start.9 = (f32[192,1024]{1,0:T(8,128)S(1)}, f32[192,1024]{1,0:T(8,128)}, u32[]{:S(2)}) copy-start(f32[192,1024]{1,0:T(8,128)} %convert_add_fusion) | copy-start | bytes 2359300
  161.3 6.4 %copy-start.10 = (f32[192,1024]{1,0:T(8,128)S(1)}, f32[192,1024]{1,0:T(8,128)}, u32[]{:S(2)}) copy-start(f32[192,1024]{1,0:T(8,128)} %convert_add_fusion.1) | copy-start | bytes 2359300
  161.3 6.4 %copy-start.16 = (f32[384,1024]{1,0:T(8,128)S(1)}, f32[384,1024]{1,0:T(8,128)}, u32[]{:S(2)}) copy-start(f32[384,1024]{1,0:T(8,128)} %fusion.144) | copy-start | bytes 4718596
  161.3 6.5 %copy-start.18 = (f32[384,384]{0,1:T(8,128)S(1)}, f32[384,384]{0,1:T(8,128)}, u32[]{:S(2)}) copy-start(f32[384,384]{0,1:T(8,128)} %copy-done.17) | copy-start | bytes 1769476
